TPU v7x, 256 devices: a whole 4x4x8 slice. The times are simulated.
256 devices in a mesh: gx: 8 (over z_hi, x), gy: 8 (over z_lo, core), gz: 4 (over y).
Axes of the slice: x: 4, y: 4, z: 8 (z_hi: 2, z_lo: 4; z = z_hi * 4 + z_lo), core: 2. Of those that a mesh axis runs over, the one named last changes fastest.
Arguments:
- tokens: bfloat16 [1024, 6144], P('gx', ('gz', 'gy')), may hold values from -6 to 6
- w_in: bfloat16 [6144, 24576], P(('gz', 'gx'), 'gy'), may hold values from -0.078125 to 0.078125
- w_out: bfloat16 [24576, 6144], P(('gy', 'gx'), 'gz'), may hold values from -0.0390625 to 0.0390625
- cotangent: bfloat16 [1024, 6144], P('gx', ('gz', 'gy')), may hold values from -1.5 to 1.5
Outputs:
- output: bfloat16 [1024, 6144], P('gx', ('gz', 'gy'))
- grad_tokens: bfloat16 [1024, 6144], P('gx', ('gz', 'gy'))
- grad_in: bfloat16 [6144, 24576], P(('gz', 'gx'), 'gy')
- grad_out: bfloat16 [24576, 6144], P(('gy', 'gx'), 'gz')
All inputs are finite; a program needn't handle non-finite values.
Results may differ from a plain program's by a relative error of at most 0.019.
Values may be sent and summed in bfloat16 or wider, within the bound.
A program may use at most 128 MiB of HBM per device.

v0:
```python
import jax
import jax.numpy as jnp
from jax import lax
from jax.sharding import PartitionSpec as P

gelu_scale = 0.7978845608


def gelu_value(pre):
    inner = gelu_scale * (pre + 0.044715 * pre * pre * pre)
    return 0.5 * pre * (1.0 + jnp.tanh(inner))


def gelu_slope(pre):
    inner = gelu_scale * (pre + 0.044715 * pre * pre * pre)
    tangent = jnp.tanh(inner)
    return 0.5 * (1.0 + tangent) + 0.5 * pre * (1.0 - tangent * tangent) * gelu_scale * (
        1.0 + 0.134145 * pre * pre
    )


def contract(left, right, left_dim, right_dim):
    return lax.dot_general(
        left, right, (((left_dim,), (right_dim,)), ((), ())), preferred_element_type=jnp.float32
    )


def on_device(tokens, w_in, w_out, cotangent):
    token_cols, cot_cols = (
        lax.all_gather(tokens, "gy", axis=1, tiled=True),
        lax.all_gather(cotangent, "gy", axis=1, tiled=True),
    )
    w_in_full = lax.all_gather(w_in, "gx", axis=0, tiled=True)
    partial_pre = jnp.dot(token_cols, w_in_full, preferred_element_type=jnp.float32)
    pre = lax.psum(partial_pre, "gz")
    act = gelu_value(pre).astype(jnp.bfloat16)
    act_rows = lax.all_to_all(act, "gx", split_axis=1, concat_axis=0, tiled=True)
    w_out_full = lax.all_gather(w_out, "gx", axis=0, tiled=True)
    output = lax.psum_scatter(
        jnp.dot(act, w_out_full, preferred_element_type=jnp.float32).astype(jnp.bfloat16),
        "gy",
        scatter_dimension=1,
        tiled=True,
    )
    partial_back = contract(cot_cols, w_out_full, 1, 1)
    left = act_rows
    grad_out = contract(left, lax.all_gather(cot_cols, "gx", axis=0, tiled=True), 0, 0).astype(
        jnp.bfloat16
    )
    back = lax.psum(partial_back, "gz")
    grad_pre = (back * gelu_slope(pre)).astype(jnp.bfloat16)
    grad_terms = contract(grad_pre, w_in_full, 1, 1)
    grad_tokens = lax.psum_scatter(grad_terms, "gy", scatter_dimension=1, tiled=True).astype(
        jnp.bfloat16
    )
    token_all = lax.all_to_all(token_cols, "gx", split_axis=1, concat_axis=0, tiled=True)
    left = token_all
    grad_in = contract(left, lax.all_gather(grad_pre, "gx", axis=0, tiled=True), 0, 0).astype(
        jnp.bfloat16
    )
    return (output, grad_tokens, grad_in, grad_out)


def solution(mesh):
    return jax.shard_map(
        on_device,
        mesh=mesh,
        in_specs=(
            P("gx", ("gz", "gy")),
            P(("gz", "gx"), "gy"),
            P(("gy", "gx"), "gz"),
            P("gx", ("gz", "gy")),
        ),
        out_specs=(
            P("gx", ("gz", "gy")),
            P("gx", ("gz", "gy")),
            P(("gz", "gx"), "gy"),
            P(("gy", "gx"), "gz"),
        ),
        check_vma=False,
    )
```

profile of v0, /device:TPU:1, one launch (start us, length us, event | category | flops | bytes accessed | tf_op | source)
XLA Modules:
  0.0 810.3 jit_solution(18336480554589738887)
XLA Ops:
  7.2 0.7 all-gather.5.cloned.1.call-update
  8.0 0.7 all-gather.7.cloned.1.call-update
  8.7 18.6 %all_gather.18 = bf16[128,1536]{0,1:T(8,128)(2,1)} all-gather(bf16[128,192]{0,1:T(8,128)(2,1)S(1)} %copy-done.2), channel_id=1, replica_groups=mesh['gx'=8,'gy'=8,'gz'=4] {'gy'}, dimensions={1}, use_global_device_ids=true | all-gather | bytes 442368 | tf_op jit(solution)/shard_map/all_gather | solution.py:30
  27.3 17.7 %all_gather.21 = bf16[128,1536]{0,1:T(8,128)(2,1)S(1)} all-gather(bf16[128,192]{0,1:T(8,128)(2,1)S(1)} %copy-done.3), channel_id=1, replica_groups=mesh['gx'=8,'gy'=8,'gz'=4] {'gy'}, dimensions={1}, use_global_device_ids=true | all-gather | bytes 442368 | tf_op jit(solution)/shard_map/all_gather | solution.py:31
  45.1 162.4 %all-gather.5.cloned.1.call-done = bf16[1536,3072]{1,0:T(8,128)(2,1)} async-done(((bf16[192,3072]{1,0:T(8,128)(2,1)}), bf16[1536,3072]{1,0:T(8,128)(2,1)}) %all-gather.5.cloned.1.call-update) | async-done | bytes 9437200 | tf_op jit(solution)/shard_map/all_gather | solution.py:33
  207.5 6.5 fusion.10
  213.9 181.1 %all-gather.7.cloned.1.call-done = bf16[3072,1536]{1,0:T(8,128)(2,1)} async-done(((bf16[384,1536]{1,0:T(8,128)(2,1)}), bf16[3072,1536]{1,0:T(8,128)(2,1)}) %all-gather.7.cloned.1.call-update) | async-done | bytes 9437200 | tf_op jit(solution)/shard_map/all_gather | solution.py:38
  395.1 8.0 fusion.11
  403.1 0.5 all-gather.11.cloned.1.call-update
  403.7 75.7 %all-reduce.3.cloned.1.call-done = (f32[128,3072]{1,0:T(8,128)}, f32[128,3072]{1,0:T(8,128)}) async-done(((f32[128,3072]{1,0:T(8,128)}, f32[128,3072]{1,0:T(8,128)}), (f32[128,3072]{1,0:T(8,128)}, f32[128,3072]{1,0:T(8,128)})) %all-reduce.3.cloned.1.call-update) | async-done | bytes 3145744 | tf_op jit(solution)/shard_map/psum | solution.py:35
  479.5 2.9 fusion.7
  482.4 7.5 fusion.12
  490.0 0.5 all-gather.9.cloned.1.call-update
  490.6 36.8 %all_to_all.38 = bf16[128,8,384]{2,0,1:T(8,128)(2,1)S(1)} all-to-all(bf16[128,8,384]{2,0,1:T(8,128)(2,1)S(1)} %bitcast.30), channel_id=1, replica_groups=mesh['gx'=8,'gy'=8,'gz'=4] {'gx'}, dimensions={1} | all-to-all | bytes 1572864 | tf_op jit(solution)/shard_map/all_to_all | solution.py:37
  527.4 4.0 all-to-all-start
  531.4 0.2 reduce-scatter.3.cloned.1.call-start
  531.7 8.2 %convolution_convert_fusion.2 = bf16[128,1536]{0,1:T(8,128)(2,1)} fusion(bf16[128,3072]{1,0:T(8,128)(2,1)S(1)} %get-tuple-element.7, bf16[3072,1536]{1,0:T(8,128)(2,1)} %all-gather.7.cloned.1.call-done), kind=kOutput, calls=%fused_computation.3 | convolution fusion | flops 1208156160 | bytes 10616832 | tf_op jit(solution)/shard_map/dot_general | solution.py:40
  539.9 51.5 %all-gather.11.cloned.1.call-done = bf16[1024,1536]{0,1:T(8,128)(2,1)} async-done(((bf16[128,1536]{0,1:T(8,128)(2,1)}), bf16[1024,1536]{0,1:T(8,128)(2,1)}) %all-gather.11.cloned.1.call-update) | async-done | bytes 3145744 | tf_op jit(solution)/shard_map/all_gather | solution.py:47
  591.4 4.3 convolution_convert_fusion.1
  595.8 32.6 %reduce-scatter.5.cloned.1.call-done = f32[128,192]{0,1:T(8,128)} async-done(((f32[128,1536]{0,1:T(8,128)}), f32[128,192]{0,1:T(8,128)}) %reduce-scatter.5.cloned.1.call-update) | async-done | bytes 98320 | tf_op jit(solution)/shard_map/reduce_scatter | solution.py:53
  628.4 1.5 convert_element_type.24
  629.9 142.4 %all-gather.9.cloned.1.call-done = bf16[1024,3072]{1,0:T(8,128)(2,1)} async-done(((bf16[128,3072]{1,0:T(8,128)(2,1)}), bf16[1024,3072]{1,0:T(8,128)(2,1)}) %all-gather.9.cloned.1.call-update) | async-done | bytes 6291472 | tf_op jit(solution)/shard_map/all_gather | solution.py:58
  772.3 5.2 fusion
  777.5 25.9 %reduce-scatter.3.cloned.1.call-done = bf16[128,192]{0,1:T(8,128)(2,1)} async-done(((bf16[128,1536]{0,1:T(8,128)(2,1)}), bf16[128,192]{0,1:T(8,128)(2,1)}) %reduce-scatter.3.cloned.1.call-update) | async-done | bytes 49168 | tf_op jit(solution)/shard_map/reduce_scatter | solution.py:39
  (19 shorter events, 0.4 us)
Async XLA Ops:
  7.2 1.6 copy-start.2
  7.2 20.1 %copy-start.3 = (bf16[128,192]{0,1:T(8,128)(2,1)S(1)}, bf16[128,192]{0,1:T(8,128)(2,1)}, u32[]{:S(2)}) copy-start(bf16[128,192]{0,1:T(8,128)(2,1)} %param.7) | copy-start | bytes 147460
  7.2 200.3 %all-gather.5.cloned.1.call-start = ((), (), s32[]{:S(2)}) async-start(), calls=%async_computation.4 | async-start | bytes 10616832 | tf_op jit(solution)/shard_map/all_gather | solution.py:33
  7.9 387.1 %all-gather.7.cloned.1.call-start = ((), (), s32[]{:S(2)}) async-start(), calls=%async_computation.5 | async-start | bytes 10616832 | tf_op jit(solution)/shard_map/all_gather | solution.py:38
  8.7 470.8 %all-reduce.3.cloned.1.call-start = ((), (), s32[]{:S(2)}) async-start(), calls=%async_computation.10 | async-start | bytes 6291456 | tf_op jit(solution)/shard_map/psum | solution.py:35
  45.1 350.0 %copy-start.1 = (bf16[128,1536]{0,1:T(8,128)(2,1)}, bf16[128,1536]{0,1:T(8,128)(2,1)S(1)}, u32[]{:S(2)}) copy-start(bf16[128,1536]{0,1:T(8,128)(2,1)S(1)} %all_gather.21) | copy-start | bytes 1179652
  403.1 188.3 %all-gather.11.cloned.1.call-start = ((), (), s32[]{:S(2)}) async-start(), calls=%async_computation.9 | async-start | bytes 3538944 | tf_op jit(solution)/shard_map/all_gather | solution.py:47
  403.7 224.7 %reduce-scatter.5.cloned.1.call-start = ((), (), s32[]{:S(2)}) async-start(), calls=%async_computation.7 | async-start | bytes 884736 | tf_op jit(solution)/shard_map/reduce_scatter | solution.py:53
  482.4 7.5 copy-start
  489.9 282.4 %all-gather.9.cloned.1.call-start = ((), (), s32[]{:S(2)}) async-start(), calls=%async_computation.8 | async-start | bytes 7077888 | tf_op jit(solution)/shard_map/all_gather | solution.py:58
  527.4 102.5 %all-to-all-start = ((bf16[128,8,192]{0,2,1:T(8,128)(2,1)}), bf16[128,8,192]{0,2,1:T(8,128)(2,1)S(1)}, u32[]{:S(2)}, u32[]{:S(2)}) async-start(bf16[128,8,192]{0,2,1:T(8,128)(2,1)} %bitcast), calls=%async_computation.2 | async-start | bytes 786432 | tf_op jit(solution)/shard_map/all_to_all | solution.py:56
  531.4 272.0 %reduce-scatter.3.cloned.1.call-start = ((), (), s32[]{:S(2)}) async-start(), calls=%async_computation.6 | async-start | bytes 442368 | tf_op jit(solution)/shard_map/reduce_scatter | solution.py:39
Sparse Core Ops, SparseCore 0:
  10.6 196.7 all-gather.4
  210.1 184.9 all-gather.6
  403.2 76.2 all-reduce.2
  482.4 109.0 all-gather.10
  594.4 33.9 reduce-scatter.4
  631.2 141.1 all-gather.8
  775.6 27.8 reduce-scatter.2
where the time goes:
time: 813 us; the launch traced here: 810 us
  waiting for transfers between devices  674 us (83%)
  blocking collectives  73.2 us (9%)
  matrix products  39.7 us (5%)
  between operations  14.2 us (2%)
    all_gather x1, waiting for transfers between devices, on_device(): w_out_full = lax.all_gather(w_out, 'gx', axis=0, tiled=True)  181 us
    all_gather x1, waiting for transfers between devices, on_device(): w_in_full = lax.all_gather(w_in, 'gx', axis=0, tiled=True)  162 us
    all_gather x1, waiting for transfers between devices, on_device(): lax.all_gather(grad_pre, 'gx', axis=0, tiled=True)  142 us
    psum x1, waiting for transfers between devices, on_device(): pre = lax.psum(partial_pre, 'gz')  75.7 us
    all_gather x1, waiting for transfers between devices, on_device(): lax.all_gather(cot_cols, 'gx', axis=0, tiled=True)  51.5 us
    all_to_all x1, blocking collectives, on_device(): lax.all_to_all(act, 'gx', split_axis=1, concat_axis=0, tiled=True)  36.8 us
    reduce_scatter x1, waiting for transfers between devices, on_device(): lax.psum_scatter(grad_terms, 'gy', scatter_dimension=1, tiled=True)  32.6 us
    reduce_scatter x1, waiting for transfers between devices, on_device(): lax.psum_scatter(jnp.dot(act, w_out_full, preferred_element_type=jnp.floa...  25.9 us
  transfers between devices with their start and end apart: 8, of which 7 were waited for; matrix products, arithmetic and copies ran while one was open for 4% of the time, Pallas kernels for 0%

commit v1 on v0

v1 whole, which is shorter than its diff:
```python
import functools

import jax
import jax.numpy as jnp
from jax import lax
from jax.experimental import pallas as pl
from jax.experimental.pallas import tpu as pltpu
from jax.sharding import PartitionSpec as P

MESH = pl.DeviceIdType.MESH
gelu_scale = 0.7978845608
bf16, f32 = jnp.bfloat16, jnp.float32


def contract(left, right, left_dim, right_dim):
    return lax.dot_general(
        left, right, (((left_dim,), (right_dim,)), ((), ())), preferred_element_type=f32
    )


def kernel(
    tok, w_in, w_out, cot, out, grad_tok, grad_in, grad_out,
    tok_sib, cot_sib, tok_piece, cot_piece, tok_all, cot_all, w_mine,
    pre_send, pre_recv, pre_sum, half_send, half_recv,
    back_send, back_recv, back_sum, act, gp,
    out_sib_send, out_sib_recv, out_own, out_x_send, out_x_recv, out_x_sum, out_z_send, out_z_recv, out_fin,
    gt_sib_send, gt_sib_recv, gt_own, gt_x_send, gt_x_recv, gt_x_sum, gt_z_send, gt_z_recv, gt_fin,
    gi_send, local_sem,
    in_ss, in_rs, w_ss, w_rs, tz_ss, tz_rs, cz_ss, cz_rs, tx_ss, tx_rs, cx_ss, cx_rs, tsib_ss, tsib_rs, csib_ss, csib_rs,
    pre_ss, pre_rs, half_ss, half_rs, back_ss, back_rs, act_ss, act_rs, gp_ss, gp_rs,
    osib_ss, osib_rs, ox_ss, ox_rs, oz_ss, oz_rs, of_ss, of_rs,
    gsib_ss, gsib_rs, gx_ss, gx_rs, gz_ss, gz_rs, gf_ss, gf_rs, gi_ss, gi_rs,
):
    ax, ay, y = lax.axis_index("gx"), lax.axis_index("gy"), lax.axis_index("gz")
    zh, x = ax // 4, lax.rem(ax, 4)
    zl, c = ay // 2, lax.rem(ay, 2)
    z = zh * 4 + zl
    oc, oh = 1 - c, 1 - zh

    def dev(x_, y_, z_, c_):
        return (z_ // 4 * 4 + x_, lax.rem(z_, 4) * 2 + c_, y_)

    def at_x(d):
        return dev(lax.rem(x + d, 4), y, z, c)

    def at_y(d):
        return dev(x, lax.rem(y + d, 4), z, c)

    def at_z(d):
        return dev(x, y, lax.rem(z + d, 8), c)

    sib = dev(x, y, z, oc)
    started = []

    def copy(src, dst, ss, rs, to):
        return pltpu.make_async_remote_copy(
            src_ref=src, dst_ref=dst, send_sem=ss, recv_sem=rs, device_id=to, device_id_type=MESH
        )

    def send(src, dst, ss, rs, to):
        one = copy(src, dst, ss, rs, to)
        one.start()
        started.append(one)
        return one

    barrier = pltpu.get_barrier_semaphore()
    peers = [at_x(d) for d in (1, 2, 3)] + [at_y(d) for d in (1, 2, 3)] + [at_z(d) for d in range(1, 8)] + [sib]
    for peer in peers:
        pl.semaphore_signal(barrier, inc=1, device_id=peer, device_id_type=MESH)
    pl.semaphore_wait(barrier, len(peers))

    other_rows = pl.ds(pl.multiple_of(oc * 64, 64), 64)
    my_rows = pl.ds(pl.multiple_of(c * 64, 64), 64)
    t_in = send(tok.at[other_rows], tok_sib, in_ss.at[0], in_rs.at[0], sib)
    c_in = send(cot.at[other_rows], cot_sib, in_ss.at[1], in_rs.at[1], sib)

    def w_cols(block, x_):
        return pl.ds(pl.multiple_of((block * 4 + x_) * 384, 384), 384)

    w_rows = pl.ds(pl.multiple_of(x * 192, 192), 192)
    w_copies = []
    for d in (2, 1, 3):
        to = lax.rem(x + d, 4)
        for b in range(2):
            w_copies.append(
                send(
                    w_in.at[:, w_cols(b, to)], w_mine.at[w_rows, pl.ds(b * 384, 384)],
                    w_ss.at[d - 1, b], w_rs.at[d - 1, b], at_x(d),
                )
            )
    for b in range(2):
        w_mine[w_rows, pl.ds(b * 384, 384)] = w_in[:, w_cols(b, x)]

    row = lax.broadcasted_iota(jnp.int32, (192, 384), 0)
    col = lax.broadcasted_iota(jnp.int32, (192, 384), 1)
    put_own = jnp.where(col == row + 192 * c, 1.0, 0.0).astype(bf16)
    put_sib = jnp.where(col == row + 192 * oc, 1.0, 0.0).astype(bf16)
    t_in.wait_recv()
    tok_piece[...] = (contract(tok[my_rows, :], put_own, 1, 0) + contract(tok_sib[...], put_sib, 1, 0)).astype(bf16)

    half = zl // 2
    t_rows = pl.ds(pl.multiple_of(c * 512 + x * 128 + zh * 64, 64), 64)
    t_cols = pl.ds(pl.multiple_of(lax.rem(zl, 2) * 384, 384), 384)
    t_slot = zh * 2 + lax.rem(zl, 2)
    t_out = []
    for j in range(4):
        mine = jnp.logical_and(half == zh, zl == j)
        one = copy(
            tok_piece, tok_all.at[t_rows, t_cols], tz_ss.at[j], tz_rs.at[t_slot], dev(x, y, half * 4 + j, c)
        )
        t_out.append((mine, one))

        @pl.when(jnp.logical_not(mine))
        def _():
            one.start()

    @pl.when(half == zh)
    def _():
        tok_all[t_rows, t_cols] = tok_piece[...]

    c_in.wait_recv()
    cot_piece[...] = (contract(cot[my_rows, :], put_own, 1, 0) + contract(cot_sib[...], put_sib, 1, 0)).astype(bf16)
    c_cols = pl.ds(pl.multiple_of(zl * 384, 384), 384)
    cz = [
        send(cot_piece, cot_all.at[t_rows, c_cols], cz_ss.at[d - 1], cz_rs.at[d - 1], at_z(d))
        for d in (4, 3, 5, 2, 6, 1, 7)
    ]
    cot_all[t_rows, c_cols] = cot_piece[...]

    for s in range(2):
        for l in range(2):
            mine = jnp.logical_and(zh == s, zl == 2 * zh + l)
            one = copy(tok_piece, tok_all.at[t_rows, t_cols], tz_ss.at[0], tz_rs.at[s * 2 + l], sib)

            @pl.when(jnp.logical_not(mine))
            def _():
                one.wait_recv()

    def x_rows(d):
        return pl.ds(pl.multiple_of(c * 512 + lax.rem(x + d, 4) * 128, 128), 128)

    def gather_x(whole, ss, rs):
        return {d: send(whole.at[x_rows(0)], whole.at[x_rows(0)], ss.at[d - 1], rs.at[d - 1], at_x(d)) for d in (2, 1, 3)}

    def to_sibling(whole, ss, rs, d):
        return send(whole.at[x_rows(d)], whole.at[x_rows(d)], ss.at[d], rs.at[d], sib)

    tx = gather_x(tok_all, tx_ss, tx_rs)
    t_sib = [to_sibling(tok_all, tsib_ss, tsib_rs, 0)]
    for one in cz:
        one.wait_recv()
    cx = gather_x(cot_all, cx_ss, cx_rs)
    c_sib = [to_sibling(cot_all, csib_ss, csib_rs, 0)]
    for d in (1, 3, 2):
        tx[d].wait_recv()
        t_sib.append(to_sibling(tok_all, tsib_ss, tsib_rs, 4 - d))
    for one in w_copies:
        one.wait_recv()
    for one in t_sib:
        one.wait_recv()

    def y_rows(d):
        return pl.ds(pl.multiple_of(lax.rem(y + d, 4) * 256, 256), 256)

    def block_cols(b):
        return pl.ds(pl.multiple_of(b * 384, 384), 384)

    pre = []
    for i, b in enumerate((oh, zh)):
        for d in (2, 1, 3):
            pre_send[i, d - 1] = contract(tok_all[y_rows(d), :], w_mine[:, block_cols(b)], 1, 0).astype(bf16)
            pre.append(
                send(pre_send.at[i, d - 1], pre_recv.at[i, d - 1], pre_ss.at[i, d - 1], pre_rs.at[i, d - 1], at_y(d))
            )
        pre_sum[i] = contract(tok_all[y_rows(0), :], w_mine[:, block_cols(b)], 1, 0)

    for one in pre[:3]:
        one.wait_recv()
    half_send[...] = (
        pre_sum[0] + pre_recv[0, 0].astype(f32) + pre_recv[0, 1].astype(f32) + pre_recv[0, 2].astype(f32)
    ).astype(bf16)
    across = send(half_send, half_recv, half_ss, half_rs, at_z(4))

    for d in (1, 3, 2):
        cx[d].wait_recv()
        c_sib.append(to_sibling(cot_all, csib_ss, csib_rs, 4 - d))
    for one in c_sib:
        one.wait_recv()
    back = []
    for d in (2, 1, 3):
        back_send[d - 1] = contract(cot_all[y_rows(d), :], w_out[...], 1, 1).astype(bf16)
        back.append(send(back_send.at[d - 1], back_recv.at[d - 1], back_ss.at[d - 1], back_rs.at[d - 1], at_y(d)))
    back_sum[...] = contract(cot_all[y_rows(0), :], w_out[...], 1, 1)

    for one in pre[3:]:
        one.wait_recv()
    pre_sum[1] = pre_sum[1] + pre_recv[1, 0].astype(f32) + pre_recv[1, 1].astype(f32) + pre_recv[1, 2].astype(f32)
    across.wait_recv()
    h = pre_sum[1] + half_recv[...].astype(f32)
    t = jnp.tanh(gelu_scale * (h + 0.044715 * h * h * h))
    act[y_rows(0), :] = (0.5 * h * (1.0 + t)).astype(bf16)
    pre_sum[0] = 0.5 * (1.0 + t) + 0.5 * h * (1.0 - t * t) * gelu_scale * (1.0 + 0.134145 * h * h)
    acts = [
        send(act.at[y_rows(0)], act.at[y_rows(0)], act_ss.at[d - 1], act_rs.at[d - 1], at_y(d)) for d in (2, 1, 3)
    ]

    for one in back:
        one.wait_recv()
    total = back_sum[...] + back_recv[0].astype(f32) + back_recv[1].astype(f32) + back_recv[2].astype(f32)
    gp[y_rows(0), block_cols(zh)] = (total * pre_sum[0]).astype(bf16)

    def gp_block(b):
        return gp.at[y_rows(0), block_cols(b)]

    gp_half = send(gp_block(zh), gp_block(zh), gp_ss.at[2, 0], gp_rs.at[2, 0], at_z(4))
    gps = [
        send(gp_block(zh), gp_block(zh), gp_ss.at[0, d - 1], gp_rs.at[0, d - 1], at_y(d)) for d in (2, 1, 3)
    ]

    def core_rows(core, i):
        return pl.ds(pl.multiple_of(core * 512 + i * 256, 256), 256)

    def scatter_sib(part, send_ref, recv_ref, own, ss, rs):
        for i in range(2):
            send_ref[pl.ds(i * 256, 256), :] = part(core_rows(oc, i)).astype(bf16)
        one = send(send_ref, recv_ref, ss, rs, sib)
        for i in range(2):
            own[pl.ds(i * 256, 256), :] = part(core_rows(c, i))
        return one

    def scatter_x(recv_ref, own, x_send, x_recv, ss, rs):
        copies = []
        for d in (2, 1, 3, 0):
            rows = pl.ds(pl.multiple_of(lax.rem(x + d, 4) * 128, 128), 128)
            both = own[rows, :] + recv_ref[rows, :].astype(f32)
            if d:
                x_send[d - 1] = both.astype(bf16)
                copies.append(send(x_send.at[d - 1], x_recv.at[d - 1], ss.at[d - 1], rs.at[d - 1], at_x(d)))
        return copies, both

    for one in acts:
        one.wait_recv()
    o_sib = scatter_sib(lambda rows: contract(act[rows, :], w_out[...], 1, 0), out_sib_send, out_sib_recv, out_own, osib_ss, osib_rs)
    o_sib.wait_recv()
    ox, mine = scatter_x(out_sib_recv, out_own, out_x_send, out_x_recv, ox_ss, ox_rs)
    out_x_sum[...] = mine

    gp_half.wait_recv()
    gps += [
        send(gp_block(oh), gp_block(oh), gp_ss.at[1, d - 1], gp_rs.at[1, d - 1], at_y(d)) for d in (2, 1, 3)
    ]

    for n in range(4):
        cols = pl.ds(n * 384, 384)
        grad_out[:, cols] = contract(act[...], cot_all[:, cols], 0, 0).astype(bf16)

    for one in ox:
        one.wait_recv()
    out_x_sum[...] = out_x_sum[...] + out_x_recv[0].astype(f32) + out_x_recv[1].astype(f32) + out_x_recv[2].astype(f32)
    out_z_send[...] = out_x_sum[...].astype(bf16)

    def z_part(ref, z_):
        rows = pl.ds(pl.multiple_of(z_ // 4 * 64, 64), 64)
        return ref.at[rows, pl.ds(pl.multiple_of(lax.rem(z_, 4) * 384, 384), 384)]

    oz = [
        send(z_part(out_z_send, lax.rem(z + d, 8)), out_z_recv.at[d - 1], oz_ss.at[d - 1], oz_rs.at[d - 1], at_z(d))
        for d in (4, 3, 5, 2, 6, 1, 7)
    ]

    for one in gps:
        one.wait_recv()
    g_sib = scatter_sib(lambda rows: contract(gp[rows, :], w_mine[...], 1, 1), gt_sib_send, gt_sib_recv, gt_own, gsib_ss, gsib_rs)
    g_sib.wait_recv()
    gx, mine = scatter_x(gt_sib_recv, gt_own, gt_x_send, gt_x_recv, gx_ss, gx_rs)
    gt_x_sum[...] = mine

    for p in range(2):
        rows = pl.ds(p * 384, 384)
        gi_send[rows, :] = contract(tok_all[:, rows], gp[...], 0, 0).astype(bf16)
    gi = []
    for d in (2, 1, 3):
        rows = pl.ds(pl.multiple_of(lax.rem(x + d, 4) * 192, 192), 192)
        for b in range(2):
            gi.append(
                send(
                    gi_send.at[rows, pl.ds(b * 384, 384)], grad_in.at[:, w_cols(b, x)],
                    gi_ss.at[d - 1, b], gi_rs.at[d - 1, b], at_x(d),
                )
            )
    for b in range(2):
        grad_in[:, w_cols(b, x)] = gi_send[w_rows, pl.ds(b * 384, 384)]

    for one in oz:
        one.wait_recv()
    total = z_part(out_x_sum, z)[...]
    for i in range(7):
        total = total + out_z_recv[i].astype(f32)
    out_fin[my_rows, :] = total.astype(bf16)
    o_fin = send(out_fin.at[my_rows], out_fin.at[my_rows], of_ss, of_rs, sib)

    for one in gx:
        one.wait_recv()
    gt_x_sum[...] = gt_x_sum[...] + gt_x_recv[0].astype(f32) + gt_x_recv[1].astype(f32) + gt_x_recv[2].astype(f32)
    gt_z_send[...] = gt_x_sum[...].astype(bf16)
    g_out = []
    for s in range(2):
        for l in range(2):
            to = s * 4 + 2 * zh + l
            mine = jnp.logical_and(zh == s, zl == 2 * zh + l)
            part = gt_z_send.at[pl.ds(s * 64, 64), pl.ds(l * 384, 384)]
            one = copy(part, gt_z_recv.at[zl], gz_ss.at[s * 2 + l], gz_rs.at[zl], dev(x, y, to, c))
            g_out.append((mine, one))

            @pl.when(jnp.logical_not(mine))
            def _():
                one.start()

            @pl.when(mine)
            def _():
                gt_z_recv[zl] = part[...]

    for j in range(4):
        mine = jnp.logical_and(half == zh, zl == j)
        one = copy(gt_z_send.at[pl.ds(0, 64), pl.ds(0, 384)], gt_z_recv.at[j], gz_ss.at[0], gz_rs.at[j], sib)

        @pl.when(jnp.logical_not(mine))
        def _():
            one.wait_recv()

    total = gt_z_recv[0].astype(f32)
    for j in range(1, 4):
        total = total + gt_z_recv[j].astype(f32)
    gt_fin[my_rows, :] = total.astype(bf16)
    g_fin = send(gt_fin.at[my_rows], gt_fin.at[my_rows], gf_ss, gf_rs, sib)

    row = lax.broadcasted_iota(jnp.int32, (384, 192), 0)
    col = lax.broadcasted_iota(jnp.int32, (384, 192), 1)
    take = jnp.where(row == col + 192 * c, 1.0, 0.0).astype(bf16)
    o_fin.wait_recv()
    out[...] = contract(out_fin[...], take, 1, 0).astype(bf16)
    g_fin.wait_recv()
    grad_tok[...] = contract(gt_fin[...], take, 1, 0).astype(bf16)
    for one in gi:
        one.wait_recv()
    for one in started:
        one.wait_send()
    for mine, one in t_out + g_out:

        @pl.when(jnp.logical_not(mine))
        def _():
            one.wait_send()


def on_device(tokens, w_in, w_out, cotangent):
    def buf(*shape, dtype=bf16):
        return pltpu.VMEM(shape, dtype)

    def sems(*shape):
        return pltpu.SemaphoreType.DMA(shape)

    dma = pltpu.SemaphoreType.DMA
    scratch = [
        buf(64, 192), buf(64, 192), buf(64, 384), buf(64, 384), buf(1024, 768), buf(1024, 1536), buf(768, 768),
        buf(2, 3, 256, 384), buf(2, 3, 256, 384), buf(2, 256, 384, dtype=f32), buf(256, 384), buf(256, 384),
        buf(3, 256, 384), buf(3, 256, 384), buf(256, 384, dtype=f32), buf(1024, 384), buf(1024, 768),
    ]
    for wide, parts in ((1536, 7), (768, 4)):
        scratch += [
            buf(512, wide), buf(512, wide), buf(512, wide, dtype=f32), buf(3, 128, wide), buf(3, 128, wide),
            buf(128, wide, dtype=f32), buf(128, wide), buf(parts, 64, 384), buf(128, 384),
        ]
    scratch += [buf(768, 768), dma]
    for shape in (
        (2,), (3, 2), (4,), (7,), (3,), (3,), (4,), (4,), (2, 3), (), (3,), (3,), (3, 3),
        (), (3,), (7,), (), (), (3,), (4,), (), (3, 2),
    ):
        scratch += [sems(*shape) if shape else dma] * 2
    shape = jax.ShapeDtypeStruct
    vmem = pl.BlockSpec(memory_space=pltpu.VMEM)
    return pl.pallas_call(
        kernel,
        out_shape=(shape((128, 192), bf16), shape((128, 192), bf16), shape((192, 3072), bf16), shape((384, 1536), bf16)),
        in_specs=[vmem] * 4,
        out_specs=[vmem] * 4,
        scratch_shapes=scratch,
        compiler_params=pltpu.CompilerParams(
            collective_id=0, has_side_effects=True, vmem_limit_bytes=58 * 1024 * 1024
        ),
        cost_estimate=pl.CostEstimate(flops=7_250_000_000, bytes_accessed=5_000_000, transcendentals=100_000),
    )(tokens, w_in, w_out, cotangent)


def solution(mesh):
    specs = (P("gx", ("gz", "gy")), P(("gz", "gx"), "gy"), P(("gy", "gx"), "gz"))
    return jax.shard_map(
        on_device,
        mesh=mesh,
        in_specs=(specs[0], specs[1], specs[2], specs[0]),
        out_specs=(specs[0], specs[0], specs[1], specs[2]),
        check_vma=False,
    )
```

time: 813 us -> 139 us (0.17)
  waiting for transfers between devices: 674 us -> 0 us
  Pallas kernels: 0 us -> 128 us
  blocking collectives: 73.2 us -> 0 us
  matrix products: 39.7 us -> 0 us
  between operations: 14.2 us -> 0.64 us
  local copies, waits for them, and re-layouts: 0.1 us -> 9.66 us
    all_gather x4 -> x0, waiting for transfers between devices: 537 us -> none  [the longest x1 181 us: on_device(): w_out_full = lax.all_gather(w_out, 'gx', axis=0, tiled=True)]
    pallas_call x0 -> x1, Pallas kernels: none -> 128 us  [on_device(): pl.pallas_call(kernel, out_shape=(shape((128, 192), bf16), shape((128, 19...]
    psum x1 -> x0, waiting for transfers between devices: 75.7 us -> none  [on_device(): pre = lax.psum(partial_pre, 'gz')]
    reduce_scatter x2 -> x0, waiting for transfers between devices: 58.5 us -> none  [the longest x1 32.6 us: on_device(): lax.psum_scatter(grad_terms, 'gy', scatter_dimension=1, tiled=True)]
    dot_general x6 -> x0, matrix products: 39.7 us -> none  [the longest x4 25 us: contract(): lax.dot_general(left, right, (((left_dim,), (right_dim,)), ((), ())), pre...]
    all_to_all x1 -> x0, blocking collectives: 36.8 us -> none  [on_device(): lax.all_to_all(act, 'gx', split_axis=1, concat_axis=0, tiled=True)]
    all_gather x2 -> x0, blocking collectives: 36.3 us -> none  [the longest x1 18.6 us: on_device(): lax.all_gather(tokens, 'gy', axis=1, tiled=True)]
  transfers between devices with their start and end apart: 8 -> 0, of which waited for: 7 -> 0; matrix products, arithmetic and copies ran while one was open for 4% -> 0% of each run, Pallas kernels for 0% -> 0%
where the time goes in v1:
time: 139 us; the launch traced here: 138 us
  Pallas kernels  128 us (92%)
  local copies, waits for them, and re-layouts  9.66 us (7%)
    pallas_call x1, Pallas kernels, on_device(): pl.pallas_call(kernel, out_shape=(shape((128, 192), bf16), shape((128, 19...  128 us
    unnamed x6, local copies, waits for them, and re-layouts  6.54 us
    pallas_call x2, local copies, waits for them, and re-layouts, on_device(): pl.pallas_call(kernel, out_shape=(shape((128, 192), bf16), shape((128, 19...  3.12 us

profile of v1, /device:TPU:1, one launch (start us, length us, event | category | flops | bytes accessed | tf_op | source)
XLA Modules:
  0.0 138.5 jit_solution(17649689205401073272)
XLA Ops:
  0.6 1.5 %copy.8.tok = bf16[128,192]{1,0:T(8,128)(2,1)} copy(bf16[128,192]{0,1:T(8,128)(2,1)} %param.4) | data formatting | bytes 98304 | tf_op args[0]
  2.2 1.5 %copy.9.cot = bf16[128,192]{1,0:T(8,128)(2,1)} copy(bf16[128,192]{0,1:T(8,128)(2,1)} %param.7) | data formatting | bytes 98304 | tf_op args[3]
  3.7 128.2 %shard_map.75 = (bf16[128,192]{1,0:T(8,128)(2,1)}, bf16[128,192]{1,0:T(8,128)(2,1)}, bf16[192,3072]{1,0:T(8,128)(2,1)}, bf16[384,1536]{1,0:T(8,128)(2,1)}) custom-call(bf16[128,192]{1,0:T(8,128)(2,1)} %copy.8.tok, bf16[192,3072]{1,0:T(8,128)(2,1)} %w_in.1, bf16[384,1536]{1,0:T(8,128)(2,1)} %w_out.1, bf16[128,192]{1,0:T(8,128)(2,1)} %copy.9.cot), custom_call_target="tpu_custom_call" | custom-call | flops 7249999872 | bytes 5000000 | tf_op jit(solution)/shard_map/pallas_call | solution.py:381
  131.9 1.6 %copy.10 = bf16[128,192]{0,1:T(8,128)(2,1)} copy(bf16[128,192]{1,0:T(8,128)(2,1)} %get-tuple-element.4) | data formatting | bytes 98304 | tf_op jit(solution)/shard_map/pallas_call | solution.py:381
  133.4 1.6 %copy.11 = bf16[128,192]{0,1:T(8,128)(2,1)} copy(bf16[128,192]{1,0:T(8,128)(2,1)} %get-tuple-element.5) | data formatting | bytes 98304 | tf_op jit(solution)/shard_map/pallas_call | solution.py:381
  135.0 0.0 copy-start
  135.0 2.5 %copy.14 = bf16[192,3072]{1,0:T(8,128)(2,1)} copy(bf16[192,3072]{1,0:T(8,128)(2,1)} %get-tuple-element.14) | data formatting | bytes 2359296
  137.4 0.0 copy-done
  137.4 1.0 copy.15
Async XLA Ops:
  135.0 2.5 %copy-start = (bf16[384,1536]{1,0:T(8,128)(2,1)S(1)}, bf16[384,1536]{1,0:T(8,128)(2,1)}, u32[]{:S(2)}) copy-start(bf16[384,1536]{1,0:T(8,128)(2,1)} %get-tuple-element.15) | copy-start | bytes 3538948

commit v2 on v0

v2 whole, which is shorter than its diff:
```python
import types

import jax
import jax.numpy as jnp
from jax import lax
from jax.experimental import pallas as pl
from jax.experimental.pallas import tpu as pltpu
from jax.sharding import PartitionSpec as P

MESH = pl.DeviceIdType.MESH
gelu_scale = 0.7978845608
bf16, f32 = jnp.bfloat16, jnp.float32


def contract(left, right, left_dim, right_dim):
    return lax.dot_general(
        left, right, (((left_dim,), (right_dim,)), ((), ())), preferred_element_type=f32
    )


def buffers():
    return dict(
        tok=((192, 128), bf16), cot=((192, 128), bf16), w_out=((384, 1536), bf16), grad_out=((384, 1536), bf16),
        tok_sib=((192, 128), bf16), cot_sib=((192, 128), bf16),
        tok_chip=((2, 4, 16, 384), bf16), cot_chip=((2, 4, 16, 384), bf16),
        tok_all=((4, 4, 64, 768), bf16), cot_all=((4, 4, 64, 1536), bf16), w_mine=((768, 768), bf16),
        pre_part=((2, 4, 4, 64, 384), f32), pre_send=((2, 4, 3, 64, 384), bf16),
        pre_fwd=((2, 4, 64, 384), bf16), pre_recv=((2, 4, 2, 64, 384), bf16),
        half_send=((4, 64, 384), bf16), half_recv=((4, 64, 384), bf16),
        back_part=((4, 256, 384), f32), back_send=((3, 256, 384), bf16),
        back_fwd=((2, 128, 384), bf16), back_recv=((2, 256, 384), bf16), slope=((256, 384), f32),
        act=((4, 256, 384), bf16), gp=((4, 256, 768), bf16),
        o_part=((4, 4, 64, 1536), f32), o_sib_send=((4, 4, 32, 1536), bf16), o_sib_recv=((4, 4, 32, 1536), bf16),
        o_own=((4, 4, 32, 1536), f32), o_ring_send=((4, 2, 4, 4, 16, 384), bf16), o_ring_recv=((4, 2, 4, 4, 16, 384), bf16),
        o_x_send=((4, 4, 16, 384), bf16), o_x_recv=((4, 3, 16, 384), bf16), o_x_own=((4, 4, 16, 384), f32),
        o_fin=((2, 4, 16, 384), bf16),
        g_part=((4, 4, 64, 768), f32), g_sib_send=((4, 4, 32, 768), bf16), g_sib_recv=((4, 4, 32, 768), bf16),
        g_own=((4, 4, 32, 768), f32), g_x_send=((4, 3, 32, 768), bf16), g_x_recv=((4, 3, 32, 768), bf16),
        g_z_send=((4, 32, 768), bf16), g_z_recv=((4, 4, 16, 384), bf16),
        g_fin=((2, 4, 16, 384), bf16), gi_send=((768, 768), bf16),
    )


def semaphores():
    return dict(
        inp=(2,), w=(3, 2), tz=(4,), cx=(3,), cz=(2, 4, 2), csib=(8, 2), tx=(3,), tsib=(4,),
        pre=(2, 4, 3), half=(4,), back=(6,), act=(4,), gp=(2, 4), gph=(4,),
        osib=(4,), oring=(4, 2, 4), ox=(4, 3), ofin=(1,),
        gsib=(4,), gx=(4, 3), gz=(4, 4), gfin=(1,), gi=(2, 3),
    )


def kernel(*refs):
    tok_hbm, w_in, w_out_hbm, cot_hbm, out, grad_tok, grad_in, grad_out_hbm = refs[:8]
    bufs = buffers()
    r = types.SimpleNamespace(**dict(zip(bufs, refs[8:])))
    rest = refs[8 + len(bufs):]
    local = rest[-1]
    sem = types.SimpleNamespace(**{name: rest[2 * i : 2 * i + 2] for i, name in enumerate(semaphores())})
    tok_all, cot_all, w_mine, act, gp = r.tok_all, r.cot_all, r.w_mine, r.act, r.gp

    ax, ay, y = lax.axis_index("gx"), lax.axis_index("gy"), lax.axis_index("gz")
    zh, x = ax // 4, lax.rem(ax, 4)
    zl, c = ay // 2, lax.rem(ay, 2)
    z = zh * 4 + zl
    oc, oh = 1 - c, 1 - zh

    def dev(x_, y_, z_, c_):
        return (z_ // 4 * 4 + x_, lax.rem(z_, 4) * 2 + c_, y_)

    def mod(v, d, n):
        return lax.rem(v + d, n)

    def at_x(d):
        return dev(mod(x, d, 4), y, z, c)

    def at_y(d):
        return dev(x, mod(y, d, 4), z, c)

    def at_z(d):
        return dev(x, y, mod(z, d, 8), c)

    sib = dev(x, y, z, oc)
    started, coming, maybe = [], [], []

    def copy(src, dst, pair, index, to, from_index=None):
        ss, rs = pair
        return pltpu.make_async_remote_copy(
            src_ref=src, dst_ref=dst, send_sem=ss.at[index], recv_sem=rs.at[index if from_index is None else from_index],
            device_id=to, device_id_type=MESH,
        )

    def send(src, dst, pair, index, to):
        one = copy(src, dst, pair, index, to)
        one.start()
        started.append(one)
        coming.append(one)
        return one

    def recv(*copies):
        for one in copies:
            one.wait_recv()
            coming[:] = [other for other in coming if other is not one]

    def send_unless(mine, one):
        maybe.append((mine, one))

        @pl.when(jnp.logical_not(mine))
        def _():
            one.start()

    def recv_unless(mine, one):
        @pl.when(jnp.logical_not(mine))
        def _():
            one.wait_recv()

    def span(i, n):
        return pl.ds(i * n if isinstance(i, int) else pl.multiple_of(i * n, n), n)

    tok, cot, w_out, grad_out = r.tok, r.cot, r.w_out, r.grad_out
    loads = []

    def load(src, dst):
        one = pltpu.make_async_copy(src, dst, local.at[len(loads)])
        one.start()
        loads.append(one)
        return one

    t_load, c_load = load(tok_hbm, tok), load(cot_hbm, cot)

    barrier = pltpu.get_barrier_semaphore()
    peers = [at_x(d) for d in (1, 2, 3)] + [at_y(d) for d in (1, 2, 3)] + [at_z(d) for d in range(1, 8)] + [sib]
    for peer in peers:
        pl.semaphore_signal(barrier, inc=1, device_id=peer, device_id_type=MESH)
    pl.semaphore_wait(barrier, len(peers))

    t_load.wait()
    c_load.wait()
    t_in = send(tok, r.tok_sib, sem.inp, 0, sib)
    c_in = send(cot, r.cot_sib, sem.inp, 1, sib)

    def w_cols(block, x_):
        return span(block * 4 + x_, 384)

    w_copies = [
        send(w_in.at[:, w_cols(b, mod(x, d, 4))], w_mine.at[span(x, 192), span(b, 384)], sem.w, (d - 1, b), at_x(d))
        for d in (2, 1, 3)
        for b in range(2)
    ]

    w_loads = [load(w_in.at[:, w_cols(b, x)], w_mine.at[span(x, 192), span(b, 384)]) for b in range(2)]
    w_out_load = load(w_out_hbm, w_out)

    row = lax.broadcasted_iota(jnp.int32, (192, 384), 0)
    col = lax.broadcasted_iota(jnp.int32, (192, 384), 1)
    put_own = jnp.where(col == row + 192 * c, 1.0, 0.0).astype(bf16)
    put_sib = jnp.where(col == row + 192 * oc, 1.0, 0.0).astype(bf16)

    def chip(own, other):
        both = contract(own[...], put_own, 0, 0) + contract(other[...], put_sib, 0, 0)
        return both.astype(bf16).reshape(2, 4, 16, 384)

    recv(t_in)
    r.tok_chip[...] = chip(tok, r.tok_sib)

    half, l_mine = zl // 2, lax.rem(zl, 2)
    my16 = span(c * 2 + zh, 16)
    t_piece, t_place = r.tok_chip.at[c], tok_all.at[:, x, my16, span(l_mine, 384)]
    for j in (0, 1, 2, 3):
        send_unless(
            jnp.logical_and(half == zh, zl == j),
            copy(t_piece, t_place, sem.tz, (j,), dev(x, y, half * 4 + j, c), (zh * 2 + l_mine,)),
        )

    @pl.when(half == zh)
    def _():
        t_place[...] = t_piece[...]

    recv(c_in)
    r.cot_chip[...] = chip(cot, r.cot_sib)
    c_piece, c_place = r.cot_chip.at[c], cot_all.at[:, x, my16, span(zl, 384)]
    cx = [send(c_piece, c_place, sem.cx, (d - 1,), at_x(d)) for d in (2, 1, 3)]
    c_place[...] = c_piece[...]

    def c_flow():
        c_sib = []

        def block(d, k):
            z_ = mod(z, d + 8, 8)
            return cot_all.at[span(k, 2), :, span(c * 2 + z_ // 4, 16), span(lax.rem(z_, 4), 384)]

        def onward(d, k, way, s):
            return send(block(d, k), block(d, k), sem.cz, (way, s, k), at_z(1 if way == 0 else 7))

        def to_sib(d, k):
            c_sib.append(send(block(d, k), block(d, k), sem.csib, (d % 8, k), sib))

        recv(*cx)
        ring = {}
        for k in range(2):
            for way in range(2):
                ring[way, k] = onward(0, k, way, 0)
        for k in range(2):
            to_sib(0, k)
        yield
        for s in range(1, 4):
            for k in range(2):
                for way in range(2):
                    recv(ring[way, k])
                    d = -s if way == 0 else s
                    if s < 3 or k == way:
                        ring[way, k] = onward(d, k, way, s)
                    to_sib(d, k)
            yield
        for k in range(2):
            recv(ring[k, k])
            to_sib(4, k)
        yield
        recv(*c_sib)
        yield

    c_steps = c_flow()
    next(c_steps)

    for s in range(2):
        for l in range(2):
            recv_unless(
                jnp.logical_and(zh == s, zl == 2 * zh + l), copy(t_piece, t_place, sem.tz, (0,), sib, (s * 2 + l,))
            )

    def t_rows(d):
        return tok_all.at[:, mod(x, d, 4), span(c, 32)]

    tx = {d: send(t_rows(0), t_rows(0), sem.tx, (d - 1,), at_x(d)) for d in (1, 3, 2)}
    t_sib = {0: send(t_rows(0), t_rows(0), sem.tsib, (0,), sib)}

    def t_arrive(d):
        recv(tx[4 - d])
        t_sib[d] = send(t_rows(d), t_rows(d), sem.tsib, (d,), sib)

    steps_x = (0, 1, 3, 2)
    blocks = (oh, zh)
    fwd, direct, joined = {}, {}, {}

    def pre_block(i):
        d = steps_x[i]
        recv(t_sib[d])
        rows = tok_all[:, mod(x, d, 4)].reshape(256, 768)
        near, far = (1, 3) if i % 2 == 0 else (3, 1)
        for b in range(2):
            r.pre_part[b, i] = contract(rows, w_mine[:, span(blocks[b], 384)], 1, 0).reshape(4, 64, 384)
            for j, to in ((0, near), (1, far)):
                whose = 2 if j == 0 else far
                r.pre_send[b, i, j] = r.pre_part[b, i, mod(y, whose, 4)].astype(bf16)
                src = r.pre_send.at[b, i, j]
                if j == 0:
                    fwd[b, i] = send(src, r.pre_fwd.at[b, i], sem.pre, (b, i, 0), at_y(to))
                else:
                    direct[b, i] = send(src, r.pre_recv.at[b, i, 0], sem.pre, (b, i, 1), at_y(to))

    def pre_join(b, i):
        near = 1 if i % 2 == 0 else 3
        recv(fwd[b, i])
        r.pre_send[b, i, 2] = (r.pre_part[b, i, mod(y, near, 4)] + r.pre_fwd[b, i].astype(f32)).astype(bf16)
        joined[b, i] = send(r.pre_send.at[b, i, 2], r.pre_recv.at[b, i, 1], sem.pre, (b, i, 2), at_y(near))

    def pre_total(b, i):
        recv(direct[b, i], joined[b, i])
        return r.pre_part[b, i, y] + r.pre_recv[b, i, 0].astype(f32) + r.pre_recv[b, i, 1].astype(f32)

    across = {}

    def pre_across(i):
        r.half_send[i] = pre_total(0, i).astype(bf16)
        across[i] = send(r.half_send.at[i], r.half_recv.at[i], sem.half, (i,), at_z(4))

    next(c_steps)
    for one in w_loads:
        one.wait()
    recv(*w_copies)
    pre_block(0)
    next(c_steps)
    t_arrive(1)
    t_arrive(3)
    pre_block(1)
    pre_join(0, 0)
    pre_join(1, 0)
    pre_block(2)
    next(c_steps)
    t_arrive(2)
    pre_join(0, 1)
    pre_join(1, 1)
    pre_block(3)
    pre_across(0)
    pre_join(0, 2)
    pre_join(1, 2)
    pre_across(1)
    next(c_steps)
    pre_join(0, 3)
    pre_join(1, 3)
    pre_across(2)
    next(c_steps)

    low, high = span(0, 128), span(1, 128)
    back_part, back_send, back_recv, back_fwd = r.back_part, r.back_send, r.back_recv, r.back_fwd
    w_out_load.wait()
    for d in (2, 1, 3, 0):
        back_part[d] = contract(cot_all[mod(y, d, 4)].reshape(256, 1536), w_out[...], 1, 1)
        if d == 2:
            back_send[1] = back_part[2].astype(bf16)
            b_low = send(back_send.at[1, low], back_fwd.at[0], sem.back, (0,), at_y(1))
            b_high = send(back_send.at[1, high], back_fwd.at[1], sem.back, (1,), at_y(3))
        elif d == 1:
            back_send[0, high] = back_part[1, high].astype(bf16)
            b_direct = [send(back_send.at[0, high], back_recv.at[0, high], sem.back, (2,), at_y(1))]
        elif d == 3:
            back_send[2, low] = back_part[3, low].astype(bf16)
            b_direct.append(send(back_send.at[2, low], back_recv.at[1, low], sem.back, (3,), at_y(3)))
    pre_across(3)
    recv(b_low)
    back_send[0, low] = (back_part[1, low] + back_fwd[0].astype(f32)).astype(bf16)
    b_direct.append(send(back_send.at[0, low], back_recv.at[0, low], sem.back, (4,), at_y(1)))
    recv(b_high)
    back_send[2, high] = (back_part[3, high] + back_fwd[1].astype(f32)).astype(bf16)
    b_direct.append(send(back_send.at[2, high], back_recv.at[1, high], sem.back, (5,), at_y(3)))

    def y_gather(ref, cols, pair, lead):
        def place(d, rows=None):
            part = mod(y, d, 4)
            return ref.at[part, :, cols] if rows is None else ref.at[part, rows, cols]

        right = send(place(0), place(0), pair, lead + (0,), at_y(1))
        left = send(place(0), place(0), pair, lead + (1,), at_y(3))
        yield
        recv(right)
        on_right = send(place(3, low), place(3, low), pair, lead + (2,), at_y(1))
        recv(left)
        on_left = send(place(1, high), place(1, high), pair, lead + (3,), at_y(3))
        yield
        recv(on_right, on_left)
        yield

    for i in range(4):
        rows = span(mod(x, steps_x[i], 4), 64)
        own = pre_total(1, i)
        recv(across[i])
        h = own + r.half_recv[i].astype(f32)
        t = jnp.tanh(gelu_scale * (h + 0.044715 * h * h * h))
        act[y, rows, :] = (0.5 * h * (1.0 + t)).astype(bf16)
        r.slope[rows, :] = 0.5 * (1.0 + t) + 0.5 * h * (1.0 - t * t) * gelu_scale * (1.0 + 0.134145 * h * h)
    a_steps = y_gather(act, slice(None), sem.act, ())
    next(a_steps)
    recv(*b_direct)
    gph = []
    my_cols, other_cols = span(zh, 384), span(oh, 384)
    for i in range(4):
        rows = span(i, 64)
        total = back_part[0, rows] + back_recv[0, rows].astype(f32) + back_recv[1, rows].astype(f32)
        gp[y, rows, my_cols] = (total * r.slope[rows, :]).astype(bf16)
        place = gp.at[y, rows, my_cols]
        gph.append(send(place, place, sem.gph, (i,), at_z(4)))
    g_own = y_gather(gp, my_cols, sem.gp, (0,))
    next(g_own)

    def o_flow(d):
        q = mod(y, d, 4)
        part, own = r.o_part.at[d], r.o_own.at[d]
        part[...] = contract(act[q], w_out[...], 1, 0).reshape(4, 64, 1536)
        r.o_sib_send[d] = part[:, span(oc, 32), :].astype(bf16)
        swap = send(r.o_sib_send.at[d], r.o_sib_recv.at[d], sem.osib, (d,), sib)
        yield
        recv(swap)
        own[...] = part[:, span(c, 32), :] + r.o_sib_recv[d].astype(f32)

        def block(e):
            z_ = mod(z, e, 8)
            return own.at[:, span(z_ // 4, 16), span(lax.rem(z_, 4), 384)]

        halves = (pl.ds(0, 2), pl.ds(2, 2))
        ring = {}
        for step in range(4):
            for way in range(2):
                to_send, got = r.o_ring_send.at[d, way, step], r.o_ring_recv.at[d, way]
                e = 4 - step if way == 0 else 4 + step
                where = halves[way] if step == 0 else slice(None)
                if step:
                    recv(ring[way])
                if step == 0:
                    to_send[where] = block(e)[where].astype(bf16)
                elif step == 1:
                    with_, without = halves[way], halves[1 - way]
                    to_send[with_] = (block(e)[with_] + got[0, with_].astype(f32)).astype(bf16)
                    to_send[without] = block(e)[without].astype(bf16)
                else:
                    to_send[...] = (block(e)[...] + got[step - 1].astype(f32)).astype(bf16)
                ring[way] = send(
                    to_send.at[where], got.at[step, where], sem.oring, (d, way, step), at_z(1 if way == 0 else 7)
                )
            yield
        recv(ring[0], ring[1])
        got = r.o_ring_recv
        r.o_x_own[d] = block(0)[...] + got[d, 0, 3].astype(f32) + got[d, 1, 3].astype(f32)
        r.o_x_send[d] = r.o_x_own[d].astype(bf16)
        ox = [
            send(r.o_x_send.at[d, mod(x, e, 4)], r.o_x_recv.at[d, e - 1], sem.ox, (d, e - 1), at_x(e)) for e in (2, 1, 3)
        ]
        yield
        recv(*ox)
        total = r.o_x_own[d, x]
        for e in range(3):
            total = total + r.o_x_recv[d, e].astype(f32)
        r.o_fin[c, q] = total.astype(bf16)
        yield

    def g_flow(d):
        q = mod(y, d, 4)
        part, own = r.g_part.at[d], r.g_own.at[d]
        part[...] = contract(gp[q], w_mine[...], 1, 1).reshape(4, 64, 768)
        r.g_sib_send[d] = part[:, span(oc, 32), :].astype(bf16)
        swap = send(r.g_sib_send.at[d], r.g_sib_recv.at[d], sem.gsib, (d,), sib)
        yield
        recv(swap)
        own[...] = part[:, span(c, 32), :] + r.g_sib_recv[d].astype(f32)
        gx = []
        for e in (2, 1, 3):
            r.g_x_send[d, e - 1] = own[mod(x, e, 4)].astype(bf16)
            gx.append(send(r.g_x_send.at[d, e - 1], r.g_x_recv.at[d, e - 1], sem.gx, (d, e - 1), at_x(e)))
        yield
        recv(*gx)
        total = own[x]
        for e in range(3):
            total = total + r.g_x_recv[d, e].astype(f32)
        r.g_z_send[d] = total.astype(bf16)
        for s in range(2):
            for l in range(2):
                mine = jnp.logical_and(zh == s, zl == 2 * zh + l)
                piece = r.g_z_send.at[d, span(s, 16), span(l, 384)]
                send_unless(
                    mine, copy(piece, r.g_z_recv.at[d, zl], sem.gz, (d, s * 2 + l), dev(x, y, s * 4 + 2 * zh + l, c), (d, zl))
                )

                @pl.when(mine)
                def _():
                    r.g_z_recv[d, zl] = piece[...]

        yield
        for j in range(4):
            recv_unless(
                jnp.logical_and(half == zh, zl == j),
                copy(r.g_z_send.at[d, span(0, 16), span(0, 384)], r.g_z_recv.at[d, j], sem.gz, (d, 0), sib, (d, j)),
            )
        total = r.g_z_recv[d, 0].astype(f32)
        for j in range(1, 4):
            total = total + r.g_z_recv[d, j].astype(f32)
        r.g_fin[c, q] = total.astype(bf16)
        yield

    gi, gi_own = [], []

    def gi_flow():
        for b, which in enumerate((zh, oh)):
            for p in range(2):
                rows = span(p, 384)
                r.gi_send[rows, span(b, 384)] = contract(
                    tok_all[:, :, :, rows].reshape(1024, 384), gp[:, :, span(which, 384)].reshape(1024, 384), 0, 0
                ).astype(bf16)
            for d in (2, 1, 3):
                gi.append(
                    send(
                        r.gi_send.at[span(mod(x, d, 4), 192), span(b, 384)], grad_in.at[:, w_cols(which, x)],
                        sem.gi, (b, d - 1), at_x(d),
                    )
                )
            gi_own.append(load(r.gi_send.at[span(x, 192), span(b, 384)], grad_in.at[:, w_cols(which, x)]))
            yield

    def go_flow():
        for n in range(4):
            cols = span(n, 384)
            grad_out[:, cols] = contract(
                act[...].reshape(1024, 384), cot_all[:, :, :, cols].reshape(1024, 384), 0, 0
            ).astype(bf16)
            yield

    def other_flow():
        recv(*gph)
        yield from y_gather(gp, other_cols, sem.gp, (1,))

    o = {d: o_flow(d) for d in range(4)}
    g = {d: g_flow(d) for d in range(4)}
    o0, o1, o2, o3 = o[0], o[1], o[2], o[3]
    g0, g1, g2, g3 = g[0], g[1], g[2], g[3]
    a, mine, other, gi_steps, go = a_steps, g_own, other_flow(), gi_flow(), go_flow()
    for flow in (o0, o0, a, o1, o1, mine, o3, o3, o0, other, g0, a, o2, g0, o2, o0, o1, mine, gi_steps, o3, other, g1, g3, g1, g3, o0, o1, o2, other, g2, g2, gi_steps, g0, o0, o1, o3, g1, g3, o2, o3, go, g2, o1, o2, go, o3, o0, g0, g1, g3, o2, go):
        next(flow)
    for flow in (g0, g1, g3, g2):
        for _ in flow:
            pass
    g_last = send(r.g_fin.at[c], r.g_fin.at[c], sem.gfin, (0,), sib)
    for flow in (o0, o1, o3, o2):
        for _ in flow:
            pass
    o_last = send(r.o_fin.at[c], r.o_fin.at[c], sem.ofin, (0,), sib)
    for _ in go:
        pass
    stored = load(grad_out, grad_out_hbm)

    row = lax.broadcasted_iota(jnp.int32, (384, 192), 0)
    col = lax.broadcasted_iota(jnp.int32, (384, 192), 1)
    take = jnp.where(row == col + 192 * c, 1.0, 0.0).astype(bf16)
    recv(o_last)
    out[...] = contract(take, r.o_fin[...].reshape(128, 384), 0, 1).astype(bf16)
    recv(g_last)
    grad_tok[...] = contract(take, r.g_fin[...].reshape(128, 384), 0, 1).astype(bf16)
    recv(*gi)
    stored.wait()
    for one in gi_own:
        one.wait()
    assert not coming
    for one in started:
        one.wait_send()
    for mine, one in maybe:

        @pl.when(jnp.logical_not(mine))
        def _():
            one.wait_send()


def hand_over(*refs):
    loads = [pltpu.make_async_copy(refs[i], refs[8 + i], refs[12].at[i]) for i in range(4)]
    stores = [pltpu.make_async_copy(refs[8 + i], refs[4 + i], refs[12].at[4 + i]) for i in range(4)]
    for one in loads:
        one.start()
    for one, then in zip(loads, stores):
        one.wait()
        then.start()
    for one in stores:
        one.wait()


def on_device(tokens, w_in, w_out, cotangent):
    scratch = [pltpu.VMEM(dims, dtype) for dims, dtype in buffers().values()]
    for dims in semaphores().values():
        scratch += [pltpu.SemaphoreType.DMA(dims)] * 2
    scratch.append(pltpu.SemaphoreType.DMA((8,)))
    shape = jax.ShapeDtypeStruct
    vmem, hbm = pl.BlockSpec(memory_space=pltpu.VMEM), pl.BlockSpec(memory_space=pl.ANY)
    shapes = (shape((192, 128), bf16), shape((192, 128), bf16), shape((192, 3072), bf16), shape((384, 1536), bf16))
    results = pl.pallas_call(
        kernel,
        out_shape=shapes,
        in_specs=[hbm] * 4,
        out_specs=[vmem, vmem, hbm, hbm],
        scratch_shapes=scratch,
        compiler_params=pltpu.CompilerParams(
            collective_id=0, has_side_effects=True, vmem_limit_bytes=60 * 1024 * 1024
        ),
        cost_estimate=pl.CostEstimate(flops=7_250_000_000, bytes_accessed=5_000_000, transcendentals=100_000),
    )(tokens.T, w_in, w_out, cotangent.T)
    out, grad_tokens, grad_in, grad_out = pl.pallas_call(
        hand_over,
        out_shape=shapes,
        in_specs=[hbm] * 4,
        out_specs=[hbm] * 4,
        scratch_shapes=[pltpu.VMEM(one.shape, one.dtype) for one in shapes] + [pltpu.SemaphoreType.DMA((8,))],
    )(*results)
    return out.T, grad_tokens.T, grad_in, grad_out


def solution(mesh):
    specs = (P("gx", ("gz", "gy")), P(("gz", "gx"), "gy"), P(("gy", "gx"), "gz"))
    return jax.shard_map(
        on_device,
        mesh=mesh,
        in_specs=(specs[0], specs[1], specs[2], specs[0]),
        out_specs=(specs[0], specs[0], specs[1], specs[2]),
        check_vma=False,
    )
```

time: 813 us -> 113 us (0.14)
  waiting for transfers between devices: 674 us -> 0 us
  Pallas kernels: 0 us -> 112 us
  blocking collectives: 73.2 us -> 0 us
  matrix products: 39.7 us -> 0 us
  between operations: 14.2 us -> 0.8 us
    all_gather x4 -> x0, waiting for transfers between devices: 537 us -> none  [the longest x1 181 us: on_device(): w_out_full = lax.all_gather(w_out, 'gx', axis=0, tiled=True)]
    pallas_call x0 -> x2, Pallas kernels: none -> 112 us  [the longest x1 109 us: on_device(): pl.pallas_call(kernel, out_shape=shapes, in_specs=[hbm] * 4, out_specs=[v...]
    psum x1 -> x0, waiting for transfers between devices: 75.7 us -> none  [on_device(): pre = lax.psum(partial_pre, 'gz')]
    reduce_scatter x2 -> x0, waiting for transfers between devices: 58.5 us -> none  [the longest x1 32.6 us: on_device(): lax.psum_scatter(grad_terms, 'gy', scatter_dimension=1, tiled=True)]
    dot_general x6 -> x0, matrix products: 39.7 us -> none  [the longest x4 25 us: contract(): lax.dot_general(left, right, (((left_dim,), (right_dim,)), ((), ())), pre...]
    all_to_all x1 -> x0, blocking collectives: 36.8 us -> none  [on_device(): lax.all_to_all(act, 'gx', split_axis=1, concat_axis=0, tiled=True)]
    all_gather x2 -> x0, blocking collectives: 36.3 us -> none  [the longest x1 18.6 us: on_device(): lax.all_gather(tokens, 'gy', axis=1, tiled=True)]
  transfers between devices with their start and end apart: 8 -> 0, of which waited for: 7 -> 0; matrix products, arithmetic and copies ran while one was open for 4% -> 0% of each run, Pallas kernels for 0% -> 0%
where the time goes in v2:
time: 113 us
  Pallas kernels  112 us (99%)
    pallas_call x1, Pallas kernels, on_device(): pl.pallas_call(kernel, out_shape=shapes, in_specs=[hbm] * 4, out_specs=[v...  109 us
    pallas_call x1, Pallas kernels, on_device(): pl.pallas_call(hand_over, out_shape=shapes, in_specs=[hbm] * 4, out_specs...  2.8 us

profile of v2, /device:TPU:1, one launch (start us, length us, event | category | flops | bytes accessed | tf_op | source)
XLA Modules:
  0.0 113.1 jit_solution(14119244970354244948)
XLA Ops:
  0.6 109.5 %shard_map.75 = (bf16[192,128]{1,0:T(8,128)(2,1)}, bf16[192,128]{1,0:T(8,128)(2,1)}, bf16[192,3072]{1,0:T(8,128)(2,1)}, bf16[384,1536]{1,0:T(8,128)(2,1)}) custom-call(bf16[192,128]{1,0:T(8,128)(2,1)} %bitcast.4, bf16[192,3072]{1,0:T(8,128)(2,1)} %refs_1_.1, bf16[384,1536]{1,0:T(8,128)(2,1)} %refs_2_.1, bf16[192,128]{1,0:T(8,128)(2,1)} %bitcast.5), custom_call_target="tpu_custom_call" | custom-call | flops 7249999872 | bytes 5000000 | tf_op jit(solution)/shard_map/pallas_call | solution.py:549
  110.1 2.8 %shard_map.76 = (bf16[192,128]{1,0:T(8,128)(2,1)}, bf16[192,128]{1,0:T(8,128)(2,1)}, bf16[192,3072]{1,0:T(8,128)(2,1)}, bf16[384,1536]{1,0:T(8,128)(2,1)}) custom-call(bf16[192,128]{1,0:T(8,128)(2,1)} %get-tuple-element.12.refs_0_, bf16[192,128]{1,0:T(8,128)(2,1)} %get-tuple-element.13.refs_1_, bf16[192,3072]{1,0:T(8,128)(2,1)} %get-tuple-element.14.refs_2_, ...), custom_call_target="tpu_custom_call" | custom-call | tf_op jit(solution)/shard_map/pallas_call | solution.py:560

commit v3 on v2

--- a/solution.py
+++ b/solution.py
@@ -144,7 +144,7 @@
 
     w_copies = [
         send(w_in.at[:, w_cols(b, mod(x, d, 4))], w_mine.at[span(x, 192), span(b, 384)], sem.w, (d - 1, b), at_x(d))
-        for d in (2, 1, 3)
+        for d in (2,)
         for b in range(2)
     ]
 
@@ -181,6 +181,12 @@
     c_piece, c_place = r.cot_chip.at[c], cot_all.at[:, x, my16, span(zl, 384)]
     cx = [send(c_piece, c_place, sem.cx, (d - 1,), at_x(d)) for d in (2, 1, 3)]
     c_place[...] = c_piece[...]
+    w_copies += [
+        send(w_in.at[:, w_cols(b, mod(x, d, 4))], w_mine.at[span(x, 192), span(b, 384)], sem.w, (d - 1, b), at_x(d))
+        for d in (1, 3)
+        for b in range(2)
+    ]
+
 
     def c_flow():
         c_sib = []

time: 113 us -> 109 us (0.965)
  Pallas kernels: 112 us -> 108 us
    pallas_call x1, Pallas kernels: 109 us -> 105 us  [on_device(): pl.pallas_call(kernel, out_shape=shapes, in_specs=[hbm] * 4, out_specs=[v...]
where the time goes in v3:
time: 109 us
  Pallas kernels  108 us (99%)
    pallas_call x1, Pallas kernels, on_device(): pl.pallas_call(kernel, out_shape=shapes, in_specs=[hbm] * 4, out_specs=[v...  105 us
    pallas_call x1, Pallas kernels, on_device(): pl.pallas_call(hand_over, out_shape=shapes, in_specs=[hbm] * 4, out_specs...  2.8 us

profile of v3, /device:TPU:1, one launch (start us, length us, event | category | flops | bytes accessed | tf_op | source)
XLA Modules:
  0.0 108.5 jit_solution(15469501410377298975)
XLA Ops:
  0.6 104.9 %shard_map.75 = (bf16[192,128]{1,0:T(8,128)(2,1)}, bf16[192,128]{1,0:T(8,128)(2,1)}, bf16[192,3072]{1,0:T(8,128)(2,1)}, bf16[384,1536]{1,0:T(8,128)(2,1)}) custom-call(bf16[192,128]{1,0:T(8,128)(2,1)} %bitcast.4, bf16[192,3072]{1,0:T(8,128)(2,1)} %refs_1_.1, bf16[384,1536]{1,0:T(8,128)(2,1)} %refs_2_.1, bf16[192,128]{1,0:T(8,128)(2,1)} %bitcast.5), custom_call_target="tpu_custom_call" | custom-call | flops 7249999872 | bytes 5000000 | tf_op jit(solution)/shard_map/pallas_call | solution.py:555
  105.6 2.8 %shard_map.76 = (bf16[192,128]{1,0:T(8,128)(2,1)}, bf16[192,128]{1,0:T(8,128)(2,1)}, bf16[192,3072]{1,0:T(8,128)(2,1)}, bf16[384,1536]{1,0:T(8,128)(2,1)}) custom-call(bf16[192,128]{1,0:T(8,128)(2,1)} %get-tuple-element.12.refs_0_, bf16[192,128]{1,0:T(8,128)(2,1)} %get-tuple-element.13.refs_1_, bf16[192,3072]{1,0:T(8,128)(2,1)} %get-tuple-element.14.refs_2_, ...), custom_call_target="tpu_custom_call" | custom-call | tf_op jit(solution)/shard_map/pallas_call | solution.py:566

commit v4 on v3

--- a/solution.py
+++ b/solution.py
@@ -142,12 +142,6 @@
     def w_cols(block, x_):
         return span(block * 4 + x_, 384)
 
-    w_copies = [
-        send(w_in.at[:, w_cols(b, mod(x, d, 4))], w_mine.at[span(x, 192), span(b, 384)], sem.w, (d - 1, b), at_x(d))
-        for d in (2,)
-        for b in range(2)
-    ]
-
     w_loads = [load(w_in.at[:, w_cols(b, x)], w_mine.at[span(x, 192), span(b, 384)]) for b in range(2)]
     w_out_load = load(w_out_hbm, w_out)
 
@@ -181,9 +175,9 @@
     c_piece, c_place = r.cot_chip.at[c], cot_all.at[:, x, my16, span(zl, 384)]
     cx = [send(c_piece, c_place, sem.cx, (d - 1,), at_x(d)) for d in (2, 1, 3)]
     c_place[...] = c_piece[...]
-    w_copies += [
+    w_copies = [
         send(w_in.at[:, w_cols(b, mod(x, d, 4))], w_mine.at[span(x, 192), span(b, 384)], sem.w, (d - 1, b), at_x(d))
-        for d in (1, 3)
+        for d in (2, 1, 3)
         for b in range(2)
     ]
 
@@ -497,7 +491,7 @@
     o0, o1, o2, o3 = o[0], o[1], o[2], o[3]
     g0, g1, g2, g3 = g[0], g[1], g[2], g[3]
     a, mine, other, gi_steps, go = a_steps, g_own, other_flow(), gi_flow(), go_flow()
-    for flow in (o0, o0, a, o1, o1, mine, o3, o3, o0, other, g0, a, o2, g0, o2, o0, o1, mine, gi_steps, o3, other, g1, g3, g1, g3, o0, o1, o2, other, g2, g2, gi_steps, g0, o0, o1, o3, g1, g3, o2, o3, go, g2, o1, o2, go, o3, o0, g0, g1, g3, o2, go):
+    for flow in (o0, o0, a, o1, o1, mine, o3, o3, o0, other, g0, a, mine, gi_steps, g0, o2, o2, o0, o1, o3, other, g1, g3, g1, g3, o0, o1, o2, other, g2, g2, gi_steps, g0, o0, o1, o3, g1, g3, o2, o3, go, g2, o1, o2, go, o3, o0, g0, g1, g3, o2, go):
         next(flow)
     for flow in (g0, g1, g3, g2):
         for _ in flow:

time: 109 us -> 107 us (0.982)
    pallas_call x1, Pallas kernels: 105 us -> 104 us  [on_device(): pl.pallas_call(kernel, out_shape=shapes, in_specs=[hbm] * 4, out_specs=[v...]
where the time goes in v4:
time: 107 us
  Pallas kernels  107 us (100%)
    pallas_call x1, Pallas kernels, on_device(): pl.pallas_call(kernel, out_shape=shapes, in_specs=[hbm] * 4, out_specs=[v...  104 us
    pallas_call x1, Pallas kernels, on_device(): pl.pallas_call(hand_over, out_shape=shapes, in_specs=[hbm] * 4, out_specs...  2.8 us

profile of v4, /device:TPU:1, one launch (start us, length us, event | category | flops | bytes accessed | tf_op | source)
XLA Modules:
  0.0 107.3 jit_solution(10325778191056518229)
XLA Ops:
  0.6 103.7 %shard_map.75 = (bf16[192,128]{1,0:T(8,128)(2,1)}, bf16[192,128]{1,0:T(8,128)(2,1)}, bf16[192,3072]{1,0:T(8,128)(2,1)}, bf16[384,1536]{1,0:T(8,128)(2,1)}) custom-call(bf16[192,128]{1,0:T(8,128)(2,1)} %bitcast.4, bf16[192,3072]{1,0:T(8,128)(2,1)} %refs_1_.1, bf16[384,1536]{1,0:T(8,128)(2,1)} %refs_2_.1, bf16[192,128]{1,0:T(8,128)(2,1)} %bitcast.5), custom_call_target="tpu_custom_call" | custom-call | flops 7249999872 | bytes 5000000 | tf_op jit(solution)/shard_map/pallas_call | solution.py:549
  104.4 2.8 %shard_map.76 = (bf16[192,128]{1,0:T(8,128)(2,1)}, bf16[192,128]{1,0:T(8,128)(2,1)}, bf16[192,3072]{1,0:T(8,128)(2,1)}, bf16[384,1536]{1,0:T(8,128)(2,1)}) custom-call(bf16[192,128]{1,0:T(8,128)(2,1)} %get-tuple-element.12.refs_0_, bf16[192,128]{1,0:T(8,128)(2,1)} %get-tuple-element.13.refs_1_, bf16[192,3072]{1,0:T(8,128)(2,1)} %get-tuple-element.14.refs_2_, ...), custom_call_target="tpu_custom_call" | custom-call | tf_op jit(solution)/shard_map/pallas_call | solution.py:560

commit v5 on v4

--- a/solution.py
+++ b/solution.py
@@ -132,30 +132,31 @@
     peers = [at_x(d) for d in (1, 2, 3)] + [at_y(d) for d in (1, 2, 3)] + [at_z(d) for d in range(1, 8)] + [sib]
     for peer in peers:
         pl.semaphore_signal(barrier, inc=1, device_id=peer, device_id_type=MESH)
-    pl.semaphore_wait(barrier, len(peers))
-
     t_load.wait()
     c_load.wait()
-    t_in = send(tok, r.tok_sib, sem.inp, 0, sib)
-    c_in = send(cot, r.cot_sib, sem.inp, 1, sib)
-
-    def w_cols(block, x_):
-        return span(block * 4 + x_, 384)
-
-    w_loads = [load(w_in.at[:, w_cols(b, x)], w_mine.at[span(x, 192), span(b, 384)]) for b in range(2)]
-    w_out_load = load(w_out_hbm, w_out)
-
     row = lax.broadcasted_iota(jnp.int32, (192, 384), 0)
     col = lax.broadcasted_iota(jnp.int32, (192, 384), 1)
     put_own = jnp.where(col == row + 192 * c, 1.0, 0.0).astype(bf16)
     put_sib = jnp.where(col == row + 192 * oc, 1.0, 0.0).astype(bf16)
+    t_own = contract(tok[...], put_own, 0, 0)
+    c_own = contract(cot[...], put_own, 0, 0)
+    pl.semaphore_wait(barrier, len(peers))
+
+    t_in = send(tok, r.tok_sib, sem.inp, 0, sib)
+    c_in = send(cot, r.cot_sib, sem.inp, 1, sib)
+
+    def w_cols(block, x_):
+        return span(block * 4 + x_, 384)
+
+    w_loads = [load(w_in.at[:, w_cols(b, x)], w_mine.at[span(x, 192), span(b, 384)]) for b in range(2)]
+    w_out_load = load(w_out_hbm, w_out)
 
     def chip(own, other):
-        both = contract(own[...], put_own, 0, 0) + contract(other[...], put_sib, 0, 0)
+        both = own + contract(other[...], put_sib, 0, 0)
         return both.astype(bf16).reshape(2, 4, 16, 384)
 
     recv(t_in)
-    r.tok_chip[...] = chip(tok, r.tok_sib)
+    r.tok_chip[...] = chip(t_own, r.tok_sib)
 
     half, l_mine = zl // 2, lax.rem(zl, 2)
     my16 = span(c * 2 + zh, 16)
@@ -171,7 +172,7 @@
         t_place[...] = t_piece[...]
 
     recv(c_in)
-    r.cot_chip[...] = chip(cot, r.cot_sib)
+    r.cot_chip[...] = chip(c_own, r.cot_sib)
     c_piece, c_place = r.cot_chip.at[c], cot_all.at[:, x, my16, span(zl, 384)]
     cx = [send(c_piece, c_place, sem.cx, (d - 1,), at_x(d)) for d in (2, 1, 3)]
     c_place[...] = c_piece[...]

time: 107 us -> 107 us (level)
  no operation moved by 1% of the time
where the time goes in v5:
time: 107 us
  Pallas kernels  106 us (99%)
    pallas_call x1, Pallas kernels, on_device(): pl.pallas_call(kernel, out_shape=shapes, in_specs=[hbm] * 4, out_specs=[v...  104 us
    pallas_call x1, Pallas kernels, on_device(): pl.pallas_call(hand_over, out_shape=shapes, in_specs=[hbm] * 4, out_specs...  2.8 us

profile of v5, /device:TPU:1, one launch (start us, length us, event | category | flops | bytes accessed | tf_op | source)
XLA Modules:
  0.0 107.3 jit_solution(1955487349079089830)
XLA Ops:
  0.6 103.7 %shard_map.75 = (bf16[192,128]{1,0:T(8,128)(2,1)}, bf16[192,128]{1,0:T(8,128)(2,1)}, bf16[192,3072]{1,0:T(8,128)(2,1)}, bf16[384,1536]{1,0:T(8,128)(2,1)}) custom-call(bf16[192,128]{1,0:T(8,128)(2,1)} %bitcast.4, bf16[192,3072]{1,0:T(8,128)(2,1)} %refs_1_.1, bf16[384,1536]{1,0:T(8,128)(2,1)} %refs_2_.1, bf16[192,128]{1,0:T(8,128)(2,1)} %bitcast.5), custom_call_target="tpu_custom_call" | custom-call | flops 7249999872 | bytes 5000000 | tf_op jit(solution)/shard_map/pallas_call | solution.py:550
  104.3 2.8 %shard_map.76 = (bf16[192,128]{1,0:T(8,128)(2,1)}, bf16[192,128]{1,0:T(8,128)(2,1)}, bf16[192,3072]{1,0:T(8,128)(2,1)}, bf16[384,1536]{1,0:T(8,128)(2,1)}) custom-call(bf16[192,128]{1,0:T(8,128)(2,1)} %get-tuple-element.12.refs_0_, bf16[192,128]{1,0:T(8,128)(2,1)} %get-tuple-element.13.refs_1_, bf16[192,3072]{1,0:T(8,128)(2,1)} %get-tuple-element.14.refs_2_, ...), custom_call_target="tpu_custom_call" | custom-call | tf_op jit(solution)/shard_map/pallas_call | solution.py:561
